TPU v7x, 512 devices: a whole 4x4x16 slice. The times are simulated.
512 devices in a mesh: tm: 8 (over x, y_hi), tile: 64 (over z, y_lo, core).
Axes of the slice: x: 4, y: 4 (y_hi: 2, y_lo: 2; y = y_hi * 2 + y_lo), z: 16, core: 2. Of those that a mesh axis runs over, the one named last changes fastest.
Arguments:
- blocks: float32 [8, 320, 128, 128], P('tm', None, 'tile'), may hold values from -16 to 16
- coef_first: float32 [128, 128], P('tile'), may hold values from 0.5 to 2
- coef_second: float32 [128, 128], P('tile'), may hold values from 0.5 to 2
- wet: int32 [128, 128], P('tile'), may hold values 0 or 1
Outputs:
- hessian: float32 [8, 320, 320], P('tm', 'tile')
All inputs are finite; a program needn't handle non-finite values. No bound on the sum of `wet` on one device may be relied on, other than what follows from the above.
Results may differ from a plain program's by a relative error of at most 0.000088.
Values sent between devices are 32-bit elements; how exact they have to be, the bound alone decides.
No kernel may reach another device: no remote copies, remote signals or barrier semaphores. Data moves between devices by JAX's collectives and lax.ppermute only.
A program may use at most 64 MiB of HBM per device.

v0:
```python
import jax
import jax.numpy as jnp
from jax import lax
from jax.sharding import Mesh
from jax.sharding import PartitionSpec as P

TILE = ("tile_0", "tile_1", "tile_2")


def extended(block, sides, width):
    for axis, dim in sides:
        count = lax.axis_size(axis)
        forward = [(i, i + 1) for i in range(count - 1)]
        backward = [(target, source) for source, target in forward]
        low = lax.ppermute(
            lax.slice_in_dim(block, block.shape[dim] - width, None, axis=dim), axis, forward
        )
        high = lax.ppermute(lax.slice_in_dim(block, 0, width, axis=dim), axis, backward)
        block = jnp.concatenate([low, block, high], axis=dim)
    return block


def reduced_to_own(blocks, axes, sequence):
    lengths = [lax.axis_size(a) for a in axes]
    blocks = blocks.reshape(*lengths, *blocks.shape[1:])
    blocks = blocks.transpose(*sequence, *range(len(axes), blocks.ndim))
    blocks = blocks.reshape(-1, *blocks.shape[len(axes) :])
    for k in sequence:
        blocks = lax.psum_scatter(blocks, axes[k], scatter_dimension=0, tiled=True)
    return blocks[0]


def split_up(array, dim, length):
    lengths = array.shape
    blocks = array.reshape(*lengths[:dim], length, lengths[dim] // length, *lengths[dim + 1 :])
    return jnp.moveaxis(blocks, dim, 0)


def summed_rows(array, axes, sequence, dim):
    length = lax.axis_size(axes)
    return reduced_to_own(split_up(array, dim, length), axes, sequence)


def sent_and_summed(array, axis, dim):
    length = lax.axis_size(axis)
    blocks = lax.all_to_all(split_up(array, dim, length), axis, 0, 0, tiled=True)
    return jnp.sum(blocks, axis=0)


def apply_sweep(wide, coef):
    inner = wide[..., 1:-1, :]
    widths = ((0, 0),) * (inner.ndim - 1) + ((1, 1),)
    padded = jnp.pad(inner, widths)
    beside = wide[..., 2:, :] + wide[..., :-2, :] + padded[..., 2:] + padded[..., :-2]
    return coef * inner + 0.2 * beside


def shards(blocks, coef_first, coef_second, wet):
    block = blocks[0]
    wetf = wet.astype(jnp.float32)
    fields = jnp.stack([coef_first, wetf])
    fields_wide = extended(fields, ((TILE, 1),), 2)
    deep = extended(block * wetf, ((TILE, 1),), 2)
    first = apply_sweep(deep, fields_wide[0][1:-1])
    second = apply_sweep(first * fields_wide[1][1:-1], coef_second)
    obs_rows = second.shape[0]
    own = second.reshape(obs_rows, second.shape[1] * second.shape[2])
    groups = lax.axis_size("tm")
    pieces = [None] * groups
    regrouped = lax.all_to_all(own[None], "tm", split_axis=2, concat_axis=0, tiled=True)
    for offset in range(groups):
        partner = jnp.roll(regrouped, -offset, axis=0)
        pieces[offset] = jnp.einsum(
            "gop,gqp->oq",
            regrouped,
            partner,
            precision=lax.Precision.HIGHEST,
            preferred_element_type=jnp.float32,
        )
    stacked = jnp.stack(pieces)
    count = jnp.float32(own.shape[1] * lax.axis_size(TILE))
    shared = summed_rows(stacked, TILE, (2, 0, 1), 1)
    mine = sent_and_summed(shared, "tm", 0)
    return mine / count


def solution(mesh):
    finer = Mesh(
        mesh.devices.reshape(mesh.shape["tm"], 16, 2, 2), ("tm", "tile_0", "tile_1", "tile_2")
    )
    in_specs = (P("tm", None, TILE, None), P(TILE, None), P(TILE, None), P(TILE, None))
    out_specs = P("tm", TILE, None)
    return jax.shard_map(
        shards, mesh=finer, in_specs=in_specs, out_specs=out_specs, check_vma=False
    )
```

profile of v0, /device:TPU:32, one launch (start us, length us, event | category | flops | bytes accessed | tf_op | source)
XLA Modules:
  0.0 220.7 jit_solution(11319167961660188351)
XLA Ops:
  7.2 1.1 bitcast_multiply_fusion
  8.3 1.9 collective-permute-start.2
  10.2 4.5 %collective-permute-start.3 = (f32[320,2,128]{2,1,0:T(2,128)S(1)}, f32[320,2,128]{2,1,0:T(2,128)S(1)}, u32[]{:S(2)}, u32[]{:S(2)}) collective-permute-start(f32[320,2,128]{2,1,0:T(2,128)S(1)} %bitcast_multiply_fusion), channel_id=1, source_target_pairs={{1,0},{2,1},{3,2},{4,3},{5,4},{6,5},{7,6},{8,7},{9,8},{10,9},{11,1... | collective-permute-start | bytes 983048 | tf_op jit(solution)/shard_map/ppermute | solution.py:18
  15.5 1.9 collective-permute-start
  17.4 4.5 %collective-permute-start.1 = (f32[2,2,128]{2,1,0:T(2,128)S(1)}, f32[2,2,128]{2,1,0:T(2,128)S(1)}, u32[]{:S(2)}, u32[]{:S(2)}) collective-permute-start(f32[2,2,128]{2,1,0:T(2,128)S(1)} %pad_maximum_fusion.5), channel_id=1, source_target_pairs={{1,0},{2,1},{3,2},{4,3},{5,4},{6,5},{7,6},{8,7},{9,8},{10,9},{11,1... | collective-permute-start | bytes 6152 | tf_op jit(solution)/shard_map/ppermute | solution.py:18
  22.0 1.3 collective-permute-done.1
  24.5 0.9 fusion.12
  27.0 16.5 %all_to_all.23 = f32[1,320,256]{1,0,2:T(1,128)S(1)} all-to-all(f32[1,320,256]{1,0,2:T(1,128)S(1)} %copy.53), channel_id=1, replica_groups=mesh['tm'=8,'tile_0'=16,'tile_1'=2,'tile_2'=2] {'tm'}, dimensions={2} | all-to-all | bytes 655360 | tf_op jit(solution)/shard_map/all_to_all | solution.py:70
  48.8 1.4 fusion.7
  50.3 2.3 %fusion.6 = f32[8,64,5,320]{3,1,2,0:T(8,128)S(1)} fusion(f32[8,64,5,320]{3,1,2,0:T(8,128)S(1)} %fusion.7, f32[64,5,8,32]{0,3,2,1:T(8,128)S(1)} %copy.55, f32[1,320,32]{1,2,0:T(8,128)} %slice_bitcast_fusion.13, f32[7,320,32]{1,2,0:T(8,128)S(1)} %get-tuple-element.6), kind=kOutput, calls=%fused_computation.15 | convolution fusion | flops 314654720 | bytes 1531904 | tf_op jit(solution)/shard_map/gop,gqp->oq/dot_general | solution.py:73
  52.5 2.5 %fusion.5 = f32[8,64,5,320]{3,1,2,0:T(8,128)S(1)} fusion(f32[8,64,5,320]{3,1,2,0:T(8,128)S(1)} %fusion.6, f32[64,5,8,32]{0,3,2,1:T(8,128)S(1)} %copy.55, f32[2,320,32]{1,2,0:T(8,128)} %get-tuple-element.8, f32[6,320,32]{1,2,0:T(8,128)} %get-tuple-element.10), kind=kOutput, calls=%fused_computation.13 | convolution fusion | flops 314654720 | bytes 1474560 | tf_op jit(solution)/shard_map/gop,gqp->oq/dot_general | solution.py:73
  55.0 1.4 fusion.4
  56.4 1.4 fusion.3
  57.9 1.4 fusion.2
  59.3 1.4 fusion.1
  60.8 1.4 fusion
  62.2 1.9 copy-done
  64.1 5.6 %reshape.89 = f32[16,2,2,8,5,320]{5,2,1,0,4,3:T(2,128)} reshape(f32[64,8,5,320]{3,0,2,1:T(8,128)} %bitcast.152) | data formatting | bytes 6553600 | tf_op jit(solution)/shard_map/reshape | solution.py:25
  69.7 6.2 %copy.64 = f32[16,2,2,8,5,320]{5,3,4,1,0,2:T(8,128)} copy(f32[16,2,2,8,5,320]{5,2,1,0,4,3:T(2,128)} %reshape.89) | data formatting | bytes 6553600 | tf_op jit(solution)/shard_map/reshape | solution.py:25
  76.0 24.5 %reduce-scatter.7.cloned.1.call-done = f32[32,8,5,320]{3,1,2,0:T(8,128)} async-done(((f32[64,8,5,320]{3,1,2,0:T(8,128)}), f32[32,8,5,320]{3,1,2,0:T(8,128)}) %reduce-scatter.7.cloned.1.call-update) | async-done | bytes 1638416 | tf_op jit(solution)/shard_map/reduce_scatter | solution.py:29
  100.6 76.6 %reduce-scatter.9.cloned.1.call-done = f32[2,8,5,320]{3,1,2,0:T(8,128)} async-done(((f32[32,8,5,320]{3,1,2,0:T(8,128)}), f32[2,8,5,320]{3,1,2,0:T(8,128)}) %reduce-scatter.9.cloned.1.call-update) | async-done | bytes 102416 | tf_op jit(solution)/shard_map/reduce_scatter | solution.py:29
  177.2 21.5 %reduce-scatter.11.cloned.1.call-done = f32[1,8,5,320]{3,1,2,0:T(8,128)} async-done(((f32[2,8,5,320]{3,1,2,0:T(8,128)}), f32[1,8,5,320]{3,1,2,0:T(8,128)}) %reduce-scatter.11.cloned.1.call-update) | async-done | bytes 51216
  198.7 0.9 copy.65
  199.5 14.0 %all_to_all.24 = f32[8,1,5,320]{3,1,2,0:T(1,128)S(1)} all-to-all(f32[8,1,5,320]{3,1,2,0:T(1,128)S(1)} %copy.65), channel_id=1, replica_groups=mesh['tm'=8,'tile_0'=16,'tile_1'=2,'tile_2'=2] {'tm'}, dimensions={0} | all-to-all | bytes 102400 | tf_op jit(solution)/shard_map/all_to_all | solution.py:46
  (46 shorter events, 10.3 us)
Async XLA Ops:
  6.5 19.0 %copy-start.7 = (f32[2,128]{1,0:T(2,128)S(1)}, f32[2,128]{1,0:T(2,128)}, u32[]{:S(2)}) copy-start(f32[2,128]{1,0:T(2,128)} %param.6) | copy-start | bytes 3076
  6.5 93.9 %reduce-scatter.7.cloned.1.call-start = ((), (), s32[]{:S(2)}) async-start(), calls=%async_computation.5 | async-start | bytes 5898240 | tf_op jit(solution)/shard_map/reduce_scatter | solution.py:29
  8.3 15.6 %collective-permute-start.2 = (f32[320,2,128]{2,1,0:T(2,128)S(1)}, f32[320,2,128]{2,1,0:T(2,128)S(1)}, u32[]{:S(2)}, u32[]{:S(2)}) collective-permute-start(f32[320,2,128]{2,1,0:T(2,128)S(1)} %bitcast_multiply_fusion), channel_id=1, source_target_pairs={{0,1},{1,2},{2,3},{3,4},{4,5},{5,6},{6,7},{7,8},{8,9},{9,10},{10,1... | collective-permute-start | bytes 983048 | tf_op jit(solution)/shard_map/ppermute | solution.py:15
  10.2 13.7 %collective-permute-start.3 = (f32[320,2,128]{2,1,0:T(2,128)S(1)}, f32[320,2,128]{2,1,0:T(2,128)S(1)}, u32[]{:S(2)}, u32[]{:S(2)}) collective-permute-start(f32[320,2,128]{2,1,0:T(2,128)S(1)} %bitcast_multiply_fusion), channel_id=1, source_target_pairs={{1,0},{2,1},{3,2},{4,3},{5,4},{6,5},{7,6},{8,7},{9,8},{10,9},{11,1... | collective-permute-start | bytes 983048 | tf_op jit(solution)/shard_map/ppermute | solution.py:18
  15.5 6.5 %collective-permute-start = (f32[2,2,128]{2,1,0:T(2,128)S(1)}, f32[2,2,128]{2,1,0:T(2,128)S(1)}, u32[]{:S(2)}, u32[]{:S(2)}) collective-permute-start(f32[2,2,128]{2,1,0:T(2,128)S(1)} %pad_maximum_fusion.5), channel_id=1, source_target_pairs={{0,1},{1,2},{2,3},{3,4},{4,5},{5,6},{6,7},{7,8},{8,9},{9,10},{10,1... | collective-permute-start | bytes 6152 | tf_op jit(solution)/shard_map/ppermute | solution.py:15
  17.4 5.8 %collective-permute-start.1 = (f32[2,2,128]{2,1,0:T(2,128)S(1)}, f32[2,2,128]{2,1,0:T(2,128)S(1)}, u32[]{:S(2)}, u32[]{:S(2)}) collective-permute-start(f32[2,2,128]{2,1,0:T(2,128)S(1)} %pad_maximum_fusion.5), channel_id=1, source_target_pairs={{1,0},{2,1},{3,2},{4,3},{5,4},{6,5},{7,6},{8,7},{9,8},{10,9},{11,1... | collective-permute-start | bytes 6152 | tf_op jit(solution)/shard_map/ppermute | solution.py:18
  48.8 6.2 %copy-start.2 = (f32[5,320,32]{1,2,0:T(8,128)S(1)}, f32[5,320,32]{1,2,0:T(8,128)}, u32[]{:S(2)}) copy-start(f32[5,320,32]{1,2,0:T(8,128)} %get-tuple-element.14) | copy-start | bytes 614404
  48.8 6.2 %copy-start.5 = (f32[3,320,32]{1,2,0:T(8,128)S(1)}, f32[3,320,32]{1,2,0:T(8,128)}, u32[]{:S(2)}) copy-start(f32[3,320,32]{1,2,0:T(8,128)} %get-tuple-element.12) | copy-start | bytes 368644
  48.8 7.6 %copy-start.3 = (f32[4,320,32]{1,2,0:T(8,128)S(1)}, f32[4,320,32]{1,2,0:T(8,128)}, u32[]{:S(2)}) copy-start(f32[4,320,32]{1,2,0:T(8,128)} %get-tuple-element.16) | copy-start | bytes 491524
  48.8 9.1 %copy-start.1 = (f32[5,320,32]{1,2,0:T(8,128)S(1)}, f32[5,320,32]{1,2,0:T(8,128)}, u32[]{:S(2)}) copy-start(f32[5,320,32]{1,2,0:T(8,128)} %get-tuple-element.13) | copy-start | bytes 614404
  48.8 9.1 %copy-start.4 = (f32[3,320,32]{1,2,0:T(8,128)S(1)}, f32[3,320,32]{1,2,0:T(8,128)}, u32[]{:S(2)}) copy-start(f32[3,320,32]{1,2,0:T(8,128)} %get-tuple-element.11) | copy-start | bytes 368644
  50.3 9.1 %copy-start.6 = (f32[2,320,32]{1,2,0:T(8,128)S(1)}, f32[2,320,32]{1,2,0:T(8,128)}, u32[]{:S(2)}) copy-start(f32[2,320,32]{1,2,0:T(8,128)} %get-tuple-element.7) | copy-start | bytes 245764
  62.2 1.9 copy-start
  75.9 101.2 %reduce-scatter.9.cloned.1.call-start = ((), (), s32[]{:S(2)}) async-start(), calls=%async_computation.6 | async-start | bytes 2088960 | tf_op jit(solution)/shard_map/reduce_scatter | solution.py:29
  100.5 98.1 %reduce-scatter.11.cloned.1.call-start = ((), (), s32[]{:S(2)}) async-start(), calls=%async_computation.7 | async-start | bytes 184320
Sparse Core Ops, SparseCore 0:
  76.0 24.3 reduce-scatter.6
  103.6 73.5 reduce-scatter.8
  179.9 18.7 reduce-scatter.10
where the time goes:
time: 221 us
  waiting for transfers between devices  124 us (56%)
  blocking collectives  30.4 us (14%)
  local copies, waits for them, and re-layouts  21.4 us (10%)
  between operations  13.4 us (6%)
  matrix products  13.3 us (6%)
  starting transfers between devices  13 us (6%)
  other arithmetic  5.33 us (2%)
    reduce_scatter x2, waiting for transfers between devices, reduced_to_own(): blocks = lax.psum_scatter(blocks, axes[k], scatter_dimension=0, tiled=True)  101 us
    unnamed x4, waiting for transfers between devices  21.5 us
    all_to_all x1, blocking collectives, shards(): lax.all_to_all(own[None], 'tm', split_axis=2, concat_axis=0, tiled=True)  16.5 us
    all_to_all x1, blocking collectives, sent_and_summed(): lax.all_to_all(split_up(array, dim, length), axis, 0, 0, tiled=True)  14 us
    dot_general x8, matrix products, shards(): jnp.einsum('gop,gqp->oq', regrouped, partner, precision=lax.Precision.HIG...  13.3 us
    reshape x2, local copies, waits for them, and re-layouts, reduced_to_own(): blocks = blocks.reshape(*lengths, *blocks.shape[1:])  11.8 us
    ppermute x2, starting transfers between devices, extended(): lax.ppermute(lax.slice_in_dim(block, 0, width, axis=dim), axis, backward)  9.08 us
    slice x8, local copies, waits for them, and re-layouts, shards(): partner = jnp.roll(regrouped, -offset, axis=0)  4.42 us
  transfers between devices with their start and end apart: 7, of which 4 were waited for; matrix products, arithmetic and copies ran while one was open for 1% of the time, Pallas kernels for 0%

commit v1 on v0

v1 whole, which is shorter than its diff:
```python
import jax
import jax.numpy as jnp
from jax import lax
from jax.experimental import pallas as pl
from jax.experimental.pallas import tpu as pltpu
from jax.sharding import Mesh
from jax.sharding import PartitionSpec as P

TM = ("xh", "xl", "yh")
TILE = ("z", "yl", "c")
LAGS, OBS, COLS = 8, 320, 128
DEPTH, QUAD = 16, 4
MINE = OBS // (DEPTH * QUAD)
PACKED = 648

VM = pl.BlockSpec(memory_space=pltpu.VMEM)


def call(body, shape, args, scratch=(), limit=16, smem=0):
    specs = [VM] * len(args)
    for i in range(smem):
        specs[len(args) - 1 - i] = pl.BlockSpec(memory_space=pltpu.SMEM)
    return pl.pallas_call(
        body,
        out_shape=jax.ShapeDtypeStruct(shape, jnp.float32),
        in_specs=specs,
        out_specs=VM,
        scratch_shapes=list(scratch),
        compiler_params=pltpu.CompilerParams(vmem_limit_bytes=limit * 2**20),
    )(*args)


def pack_body(block_ref, coef_ref, second_ref, wet_ref, out_ref, wet_in, sems):
    copies = [
        pltpu.make_async_copy(src, to, sems.at[i])
        for i, (src, to) in enumerate(
            (
                (wet_ref, wet_in),
                (coef_ref, out_ref.at[2 * OBS : 2 * OBS + 2]),
                (second_ref, out_ref.at[2 * OBS + 4 : 2 * OBS + 6]),
                (block_ref, out_ref.at[0 : 2 * OBS]),
            )
        )
    ]
    for copy in copies:
        copy.start()
    for copy in copies:
        copy.wait()
    wet = wet_in[...].astype(jnp.float32)
    both = jnp.concatenate([wet] * 4, axis=0)
    for i in range(0, 2 * OBS, 8):
        out_ref[i : i + 8, :] = out_ref[i : i + 8, :] * both
    out_ref[2 * OBS + 2 : 2 * OBS + 4, :] = wet
    out_ref[2 * OBS + 6 :, :] = jnp.zeros((2, COLS), jnp.float32)


def smooth_body(own_ref, up_ref, down_ref, out_ref):
    lane = lax.broadcasted_iota(jnp.int32, (1, COLS), 1)
    fifth_l = jnp.where(lane > 0, 0.2, 0.0).astype(jnp.float32)
    fifth_r = jnp.where(lane < COLS - 1, 0.2, 0.0).astype(jnp.float32)

    def lateral(u):
        return pltpu.roll(u, 1, 1) * fifth_l + pltpu.roll(u, COLS - 1, 1) * fifth_r

    def row(ref, i):
        return ref[2 * OBS + i : 2 * OBS + i + 1, :]

    coef = [row(up_ref, 1), row(own_ref, 0), row(own_ref, 1), row(down_ref, 0)]
    wet = [row(up_ref, 3), row(own_ref, 2), row(own_ref, 3), row(down_ref, 2)]
    late = [row(own_ref, 4), row(own_ref, 5)]
    n = 32
    for o in range(0, OBS, n):
        rows = [
            ref[pl.ds(2 * o + r, n, 2), :]
            for ref in (up_ref, own_ref, down_ref)
            for r in (0, 1)
        ]
        first = []
        for i in range(4):
            mid = rows[i + 1]
            total = coef[i] * mid + 0.2 * (rows[i] + rows[i + 2]) + lateral(mid)
            first.append(total * wet[i])
        for r in range(2):
            mid = first[r + 1]
            value = late[r] * mid + 0.2 * (first[r] + first[r + 2]) + lateral(mid)
            for t in range(LAGS):
                if t // 2 % 2 == r:
                    out_ref[t, o : o + n, :] = value


def lag_body(all_ref, shift_ref, out_ref, hi_ref, lo_ref, acc_ref):
    for g in range(LAGS):
        full = all_ref[g]
        hi = full.astype(jnp.bfloat16)
        lo = (full - hi.astype(jnp.float32)).astype(jnp.bfloat16)
        before = (g + LAGS - 1) % LAGS
        for ref, value in ((hi_ref, hi), (lo_ref, lo)):
            ref[g, :, 0:COLS] = value
            ref[before, :, COLS : 2 * COLS] = value

    def product(a, b):
        return lax.dot_general(
            a, b, (((1,), (1,)), ((), ())), preferred_element_type=jnp.float32
        )

    half = DEPTH // 2 * MINE
    for pick in range(2):
        total = None
        for g in range(0, LAGS, 2):
            partner = lax.rem(shift_ref[0] + (2 * pick + g), LAGS)
            hi, lo = hi_ref[g], lo_ref[g]
            hi_p, lo_p = hi_ref[partner], lo_ref[partner]
            term = product(hi, hi_p) + (product(hi, lo_p) + product(lo, hi_p))
            total = term if total is None else total + term
        acc_ref[...] = total
        for q in range(QUAD):
            to_q = pick * QUAD + q
            for z in range(DEPTH):
                src = slice((z * QUAD + q) * MINE, (z * QUAD + q + 1) * MINE)
                to = z * MINE
                out_ref[to_q, to : to + MINE, :] = acc_ref[src, 0:128]
                out_ref[to_q, 2 * half + to : 2 * half + to + MINE, :] = acc_ref[src, 128:256]
                to, side = (to % half) + 4 * half, (to // half) * 64
                out_ref[to_q, to : to + MINE, side : side + 64] = acc_ref[src, 256:320]


def summed(parts):
    while len(parts) > 1:
        parts = [a + b for a, b in zip(parts[::2], parts[1::2])]
    return parts[0]


def quad_body(in_ref, out_ref):
    half = DEPTH // 2 * MINE
    total = summed([in_ref[i] for i in range(2 * QUAD)])
    left, mid, last = total[: 2 * half], total[2 * half : 4 * half], total[4 * half :]
    swapped = pltpu.roll(last, 64, 1)
    for z in range(DEPTH):
        to = z * MINE
        out_ref[z, 0:MINE, :] = left[to : to + MINE]
        out_ref[z, MINE : 2 * MINE, :] = mid[to : to + MINE]
        side = last if to < half else swapped
        out_ref[z, 2 * MINE : 3 * MINE, :] = side[to % half : to % half + MINE]
        out_ref[z, 3 * MINE :, :] = jnp.zeros((1, 128), jnp.float32)


def final_body(in_ref, out_ref):
    total = summed([in_ref[i] for i in range(DEPTH)]) * (1.0 / 16384.0)
    out_ref[:, 0, 0:128] = total[0:MINE]
    out_ref[:, 0, 128:256] = total[MINE : 2 * MINE]
    out_ref[:, 0, 256:320] = total[2 * MINE : 3 * MINE, 0:64]


def shards(blocks, coef_first, coef_second, wet):
    own = pl.pallas_call(
        pack_body,
        out_shape=jax.ShapeDtypeStruct((PACKED, COLS), jnp.float32),
        in_specs=[pl.BlockSpec(memory_space=pltpu.HBM)] * 4,
        out_specs=VM,
        scratch_shapes=[pltpu.VMEM((2, COLS), jnp.int32), pltpu.SemaphoreType.DMA((4,))],
        compiler_params=pltpu.CompilerParams(vmem_limit_bytes=4 * 2**20),
    )(blocks.reshape(2 * OBS, COLS), coef_first, coef_second, wet)
    shift = 4 * lax.axis_index("xh") + lax.axis_index("yh")
    shift = shift.astype(jnp.int32).reshape(1)
    own, shift = lax.optimization_barrier((own, shift))
    count = lax.axis_size(TILE)
    up = lax.ppermute(own, TILE, [(i, i + 1) for i in range(count - 1)])
    down = lax.ppermute(own, TILE, [(i + 1, i) for i in range(count - 1)])
    spread = call(smooth_body, (LAGS, OBS, COLS), (own, up, down))
    every = lax.all_to_all(spread, TM, 0, 0, tiled=True)
    part = call(
        lag_body,
        (2 * QUAD, OBS * OBS // QUAD // 128, 128),
        (every, shift),
        [
            pltpu.VMEM((LAGS, OBS, 2 * COLS), jnp.bfloat16),
            pltpu.VMEM((LAGS, OBS, 2 * COLS), jnp.bfloat16),
            pltpu.VMEM((OBS, OBS), jnp.float32),
        ],
        smem=1,
    )
    part = lax.all_to_all(part, ("xl", "yl", "c"), 0, 0, tiled=True)
    part = call(quad_body, (DEPTH, 16, 128), (part,))
    part = lax.all_to_all(part, "z", 0, 0, tiled=True)
    return call(final_body, (MINE, 1, OBS), (part,)).reshape(1, MINE, OBS)


def solution(mesh):
    finer = Mesh(mesh.devices.reshape(2, 2, 2, 16, 2, 2), TM + TILE)
    in_specs = (P(TM, None, TILE, None), P(TILE, None), P(TILE, None), P(TILE, None))
    return jax.shard_map(
        shards, mesh=finer, in_specs=in_specs, out_specs=P(TM, TILE, None), check_vma=False
    )
```

time: 221 us -> 90.7 us (0.41)
  waiting for transfers between devices: 124 us -> 7.51 us
  blocking collectives: 30.4 us -> 70.8 us
  local copies, waits for them, and re-layouts: 21.4 us -> 3.01 us
  between operations: 13.4 us -> 0.05 us
  matrix products: 13.3 us -> 0 us
  starting transfers between devices: 13 us -> 4.39 us
  other arithmetic: 5.33 us -> 0 us
  Pallas kernels: 0 us -> 4.57 us
    reduce_scatter x2 -> x0, waiting for transfers between devices: 101 us -> none  [reduced_to_own(): blocks = lax.psum_scatter(blocks, axes[k], scatter_dimension=0, tiled=True)]
    all_to_all x2 -> x3, blocking collectives: 30.4 us -> 70.8 us  [the longest x1 29 us: shards(): part = lax.all_to_all(part, 'z', 0, 0, tiled=True)]
    unnamed x4 -> x0, waiting for transfers between devices: 21.5 us -> none
    dot_general x8 -> x0, matrix products: 13.3 us -> none  [shards(): jnp.einsum('gop,gqp->oq', regrouped, partner, precision=lax.Precision.HIG...]
    reshape x2 -> x0, local copies, waits for them, and re-layouts: 11.8 us -> none  [reduced_to_own(): blocks = blocks.reshape(*lengths, *blocks.shape[1:])]
    ppermute x4 -> x2, starting transfers between devices: 12.9 us -> 4.39 us  [the longest x1 2.47 us: shards(): down = lax.ppermute(own, TILE, [(i + 1, i) for i in range(count - 1)])]
    ppermute x4 -> x2, waiting for transfers between devices: 1.28 us -> 7.51 us  [the longest x1 4.83 us: shards(): up = lax.ppermute(own, TILE, [(i, i + 1) for i in range(count - 1)])]
    slice x9 -> x0, local copies, waits for them, and re-layouts: 4.59 us -> none  [the longest x8 4.42 us: shards(): partner = jnp.roll(regrouped, -offset, axis=0)]
  transfers between devices with their start and end apart: 7 -> 2, of which waited for: 4 -> 2; matrix products, arithmetic and copies ran while one was open for 1% -> 0% of each run, Pallas kernels for 0% -> 0%
where the time goes in v1:
time: 90.7 us; the launch traced here: 90.4 us
  blocking collectives  70.8 us (78%)
  waiting for transfers between devices  7.51 us (8%)
  Pallas kernels  4.57 us (5%)
  starting transfers between devices  4.39 us (5%)
  local copies, waits for them, and re-layouts  3.01 us (3%)
    all_to_all x1, blocking collectives, shards(): part = lax.all_to_all(part, 'z', 0, 0, tiled=True)  29 us
    all_to_all x1, blocking collectives, shards(): every = lax.all_to_all(spread, TM, 0, 0, tiled=True)  26.5 us
    all_to_all x1, blocking collectives, shards(): part = lax.all_to_all(part, ('xl', 'yl', 'c'), 0, 0, tiled=True)  15.3 us
    ppermute x1, waiting for transfers between devices, shards(): up = lax.ppermute(own, TILE, [(i, i + 1) for i in range(count - 1)])  4.83 us
    pallas_call x4, Pallas kernels, call(): pl.pallas_call(body, out_shape=jax.ShapeDtypeStruct(shape, jnp.float32),...  4.4 us
    unnamed x8, local copies, waits for them, and re-layouts  3.01 us
    ppermute x1, waiting for transfers between devices, shards(): down = lax.ppermute(own, TILE, [(i + 1, i) for i in range(count - 1)])  2.69 us
    ppermute x1, starting transfers between devices, shards(): down = lax.ppermute(own, TILE, [(i + 1, i) for i in range(count - 1)])  2.47 us
  transfers between devices with their start and end apart: 2, of which 2 were waited for; matrix products, arithmetic and copies ran while one was open for 0% of the time, Pallas kernels for 0%

profile of v1, /device:TPU:32, one launch (start us, length us, event | category | flops | bytes accessed | tf_op | source)
XLA Modules:
  0.0 90.4 jit_solution(3630067868242400351)
XLA Ops:
  0.0 0.0 copy-start
  0.0 1.0 %copy-done = f32[1,320,2,128]{3,2,1,0:T(2,128)S(1)} copy-done((f32[1,320,2,128]{3,2,1,0:T(2,128)S(1)}, f32[1,320,2,128]{3,2,1,0:T(2,128)}, u32[]{:S(2)}) %copy-start) | copy-done | bytes 327704
  1.0 0.0 copy-start.1
  1.0 0.7 copy-done.1
  1.7 0.0 copy-start.2
  1.7 0.7 copy-done.2
  2.3 0.0 copy-start.3
  2.3 0.7 copy-done.3
  3.0 0.2 shard_map.46.own_ref
  3.2 2.5 %collective-permute-start.1 = (f32[648,128]{1,0:T(8,128)S(1)}, f32[648,128]{1,0:T(8,128)S(1)}, u32[]{:S(2)}, u32[]{:S(2)}) collective-permute-start(f32[648,128]{1,0:T(8,128)S(1)} %shard_map.46.own_ref), channel_id=1, source_target_pairs={{1,0},{2,1},{3,2},{4,3},{5,4},{6,5},{7,6},{8,7},{9,8},{10,9},{11,1... | collective-permute-start | bytes 995336 | tf_op jit(solution)/shard_map/ppermute | solution.py:168
  5.7 1.9 %collective-permute-start = (f32[648,128]{1,0:T(8,128)S(1)}, f32[648,128]{1,0:T(8,128)S(1)}, u32[]{:S(2)}, u32[]{:S(2)}) collective-permute-start(f32[648,128]{1,0:T(8,128)S(1)} %shard_map.46.own_ref), channel_id=1, source_target_pairs={{0,1},{1,2},{2,3},{3,4},{4,5},{5,6},{6,7},{7,8},{8,9},{9,10},{10,1... | collective-permute-start | bytes 995336 | tf_op jit(solution)/shard_map/ppermute | solution.py:167
  7.6 2.7 %collective-permute-done.1.down_ref = f32[648,128]{1,0:T(8,128)S(1)} collective-permute-done((f32[648,128]{1,0:T(8,128)S(1)}, f32[648,128]{1,0:T(8,128)S(1)}, u32[]{:S(2)}, u32[]{:S(2)}) %collective-permute-start.1) | collective-permute-done | bytes 331808 | tf_op jit(solution)/shard_map/ppermute | solution.py:168
  10.3 4.8 %collective-permute-done.up_ref = f32[648,128]{1,0:T(8,128)S(1)} collective-permute-done((f32[648,128]{1,0:T(8,128)S(1)}, f32[648,128]{1,0:T(8,128)S(1)}, u32[]{:S(2)}, u32[]{:S(2)}) %collective-permute-start) | collective-permute-done | bytes 331808 | tf_op jit(solution)/shard_map/ppermute | solution.py:167
  15.1 1.0 %shard_map.47 = f32[8,320,128]{2,1,0:T(8,128)S(1)} custom-call(f32[648,128]{1,0:T(8,128)S(1)} %shard_map.46.own_ref, f32[648,128]{1,0:T(8,128)S(1)} %collective-permute-done.up_ref, f32[648,128]{1,0:T(8,128)S(1)} %collective-permute-done.1.down_ref), custom_call_target="tpu_custom_call" | custom-call | tf_op jit(solution)/shard_map/pallas_call | solution.py:23
  16.1 26.5 %all_to_all.15.all_ref = f32[8,320,128]{2,1,0:T(8,128)S(1)} all-to-all(f32[8,320,128]{2,1,0:T(8,128)S(1)} %shard_map.47), channel_id=1, replica_groups=mesh['xh'=2,'xl'=2,'yh'=2,'z'=16,'yl'=2,'c'=2] {'xh','xl','yh'}, dimensions={0} | all-to-all | bytes 2621440 | tf_op jit(solution)/shard_map/all_to_all | solution.py:170
  42.6 2.7 %shard_map.48 = f32[8,200,128]{2,1,0:T(8,128)S(1)} custom-call(f32[8,320,128]{2,1,0:T(8,128)S(1)} %all_to_all.15.all_ref, s32[1]{0:T(128)} %bitcast.1.shift_ref), custom_call_target="tpu_custom_call" | custom-call | tf_op jit(solution)/shard_map/pallas_call | solution.py:23
  45.3 15.3 %all_to_all.16.in_ref = f32[8,200,128]{2,1,0:T(8,128)S(1)} all-to-all(f32[8,200,128]{2,1,0:T(8,128)S(1)} %shard_map.48), channel_id=1, replica_groups=mesh['xh'=2,'xl'=2,'yh'=2,'z'=16,'yl'=2,'c'=2] {'xl','yl','c'}, dimensions={0} | all-to-all | bytes 1638400 | tf_op jit(solution)/shard_map/all_to_all | solution.py:182
  60.6 0.1 shard_map.49
  60.7 29.0 %all_to_all.17.in_ref = f32[16,16,128]{2,1,0:T(8,128)S(1)} all-to-all(f32[16,16,128]{2,1,0:T(8,128)S(1)} %shard_map.49), channel_id=1, replica_groups=mesh['xh'=2,'xl'=2,'yh'=2,'z'=16,'yl'=2,'c'=2] {'z'}, dimensions={0} | all-to-all | bytes 262144 | tf_op jit(solution)/shard_map/all_to_all | solution.py:184
  89.8 0.6 shard_map.50
Async XLA Ops:
  0.0 1.0 %copy-start = (f32[1,320,2,128]{3,2,1,0:T(2,128)S(1)}, f32[1,320,2,128]{3,2,1,0:T(2,128)}, u32[]{:S(2)}) copy-start(f32[1,320,2,128]{3,2,1,0:T(2,128)} %param.4) | copy-start | bytes 983044
  1.0 0.7 copy-start.1
  1.7 0.7 copy-start.2
  2.3 0.7 copy-start.3
  3.2 7.1 %collective-permute-start.1 = (f32[648,128]{1,0:T(8,128)S(1)}, f32[648,128]{1,0:T(8,128)S(1)}, u32[]{:S(2)}, u32[]{:S(2)}) collective-permute-start(f32[648,128]{1,0:T(8,128)S(1)} %shard_map.46.own_ref), channel_id=1, source_target_pairs={{1,0},{2,1},{3,2},{4,3},{5,4},{6,5},{7,6},{8,7},{9,8},{10,9},{11,1... | collective-permute-start | bytes 995336 | tf_op jit(solution)/shard_map/ppermute | solution.py:168
  5.7 9.4 %collective-permute-start = (f32[648,128]{1,0:T(8,128)S(1)}, f32[648,128]{1,0:T(8,128)S(1)}, u32[]{:S(2)}, u32[]{:S(2)}) collective-permute-start(f32[648,128]{1,0:T(8,128)S(1)} %shard_map.46.own_ref), channel_id=1, source_target_pairs={{0,1},{1,2},{2,3},{3,4},{4,5},{5,6},{6,7},{7,8},{8,9},{9,10},{10,1... | collective-permute-start | bytes 995336 | tf_op jit(solution)/shard_map/ppermute | solution.py:167

commit v2 on v1

v2 whole, which is shorter than its diff:
```python
import jax
import jax.numpy as jnp
from jax import lax
from jax.experimental import pallas as pl
from jax.experimental.pallas import tpu as pltpu
from jax.sharding import Mesh
from jax.sharding import PartitionSpec as P

TM = ("xh", "xl", "yh")
TILE = ("z", "yl", "c")
LAGS, OBS, COLS = 8, 320, 128
DEPTH, QUAD = 16, 4
MINE = OBS // (DEPTH * QUAD)
PACKED = 648

VM = pl.BlockSpec(memory_space=pltpu.VMEM)


def call(body, shape, args, scratch=(), limit=16, smem=0):
    specs = [VM] * (len(args) - smem) + [pl.BlockSpec(memory_space=pltpu.SMEM)] * smem
    return pl.pallas_call(
        body,
        out_shape=jax.ShapeDtypeStruct(shape, jnp.float32),
        in_specs=specs,
        out_specs=VM,
        scratch_shapes=list(scratch),
        compiler_params=pltpu.CompilerParams(vmem_limit_bytes=limit * 2**20),
    )(*args)


def pack_body(block_ref, fields_ref, out_ref):
    wet = fields_ref[2:4, :]
    both = jnp.concatenate([wet] * 4, axis=0)
    for i in range(0, 2 * OBS, 8):
        out_ref[i : i + 8, :] = block_ref[i : i + 8, :] * both
    out_ref[2 * OBS :, :] = fields_ref[...]


def smooth_body(own_ref, near_ref, far_ref, core_ref, out_ref):
    @pl.when(core_ref[0] == 0)
    def _():
        smooth(own_ref, far_ref, near_ref, out_ref)

    @pl.when(core_ref[0] == 1)
    def _():
        smooth(own_ref, near_ref, far_ref, out_ref)


def smooth(own_ref, up_ref, down_ref, out_ref):
    lane = lax.broadcasted_iota(jnp.int32, (1, COLS), 1)
    fifth_l = jnp.where(lane > 0, 0.2, 0.0).astype(jnp.float32)
    fifth_r = jnp.where(lane < COLS - 1, 0.2, 0.0).astype(jnp.float32)

    def lateral(u):
        return pltpu.roll(u, 1, 1) * fifth_l + pltpu.roll(u, COLS - 1, 1) * fifth_r

    def row(ref, i):
        return ref[2 * OBS + i : 2 * OBS + i + 1, :]

    coef = [row(up_ref, 1), row(own_ref, 0), row(own_ref, 1), row(down_ref, 0)]
    wet = [row(up_ref, 3), row(own_ref, 2), row(own_ref, 3), row(down_ref, 2)]
    late = [row(own_ref, 4), row(own_ref, 5)]
    n = 32
    for o in range(0, OBS, n):
        rows = [
            ref[pl.ds(2 * o + r, n, 2), :]
            for ref in (up_ref, own_ref, down_ref)
            for r in (0, 1)
        ]
        first = []
        for i in range(4):
            mid = rows[i + 1]
            total = coef[i] * mid + 0.2 * (rows[i] + rows[i + 2]) + lateral(mid)
            first.append(total * wet[i])
        for r in range(2):
            mid = first[r + 1]
            value = late[r] * mid + 0.2 * (first[r] + first[r + 2]) + lateral(mid)
            for t in range(LAGS):
                if t // 2 % 2 == r:
                    out_ref[t, o : o + n, :] = value


def lag_body(all_ref, shift_ref, out_ref, hi_ref, lo_ref, acc_ref):
    for g in range(LAGS):
        full = all_ref[g]
        hi = full.astype(jnp.bfloat16)
        lo = (full - hi.astype(jnp.float32)).astype(jnp.bfloat16)
        before = (g + LAGS - 1) % LAGS
        for ref, value in ((hi_ref, hi), (lo_ref, lo)):
            ref[g, :, 0:COLS] = value
            ref[before, :, COLS : 2 * COLS] = value

    def product(a, b):
        return lax.dot_general(
            a, b, (((1,), (1,)), ((), ())), preferred_element_type=jnp.float32
        )

    total = None
    for g in range(0, LAGS, 2):
        hi, lo = hi_ref[g], lo_ref[g]
        right = []
        for pick in range(2):
            partner = lax.rem(shift_ref[0] + (2 * pick + g), LAGS)
            hi_p, lo_p = hi_ref[partner], lo_ref[partner]
            right.append(jnp.concatenate([hi_p, lo_p, hi_p], axis=1))
        term = product(jnp.concatenate([hi, hi, lo], axis=1), jnp.concatenate(right, axis=0))
        total = term if total is None else total + term
    acc_ref[0] = total[:, 0:OBS]
    acc_ref[1] = total[:, OBS : 2 * OBS]
    half = DEPTH // 2 * MINE
    for pick in range(2):
        for q in range(QUAD):
            to_q = pick * QUAD + q
            for z in range(DEPTH):
                src = slice((z * QUAD + q) * MINE, (z * QUAD + q + 1) * MINE)
                to = z * MINE
                out_ref[to_q, to : to + MINE, :] = acc_ref[pick, src, 0:128]
                out_ref[to_q, 2 * half + to : 2 * half + to + MINE, :] = acc_ref[pick, src, 128:256]
                to, side = (to % half) + 4 * half, (to // half) * 64
                out_ref[to_q, to : to + MINE, side : side + 64] = acc_ref[pick, src, 256:320]


def summed(parts):
    while len(parts) > 1:
        parts = [a + b for a, b in zip(parts[::2], parts[1::2])]
    return parts[0]


def quad_body(in_ref, out_ref):
    half = DEPTH // 2 * MINE
    total = summed([in_ref[i] for i in range(2 * QUAD)])
    left, mid, last = total[: 2 * half], total[2 * half : 4 * half], total[4 * half :]
    swapped = pltpu.roll(last, 64, 1)
    for z in range(DEPTH):
        to = z * MINE
        side = last if to < half else swapped
        for i in range(MINE):
            row = to + i
            out_ref[z, :, i * OBS : i * OBS + 128] = left[row : row + 1]
            out_ref[z, :, i * OBS + 128 : i * OBS + 256] = mid[row : row + 1]
            row = row % half
            out_ref[z, :, i * OBS + 256 : i * OBS + 320] = side[row : row + 1, 0:64]


def final_body(in_ref, out_ref):
    total = summed([in_ref[i] for i in range(DEPTH)]) * (1.0 / 16384.0)
    for i in range(MINE):
        out_ref[i] = total[:, i * OBS : (i + 1) * OBS]


def shards(blocks, coef_first, coef_second, wet):
    fields = (coef_first, wet, coef_second)
    fields = sum(
        jnp.pad(f, ((2 * i, 6 - 2 * i), (0, 0))).astype(jnp.float32) for i, f in enumerate(fields)
    )
    own = call(pack_body, (PACKED, COLS), (blocks.reshape(2 * OBS, COLS), fields), limit=4)
    shift = 4 * lax.axis_index("xh") + lax.axis_index("yh")
    shift = shift.astype(jnp.int32).reshape(1)
    core = lax.axis_index("c").astype(jnp.int32).reshape(1)
    own, shift, core = lax.optimization_barrier((own, shift, core))
    pairs = [(i, i + 1) for i in range(1, lax.axis_size(TILE) - 1, 2)]
    far = lax.ppermute(own, TILE, pairs + [(b, a) for a, b in pairs])
    near = lax.ppermute(own, "c", [(0, 1), (1, 0)])
    spread = call(smooth_body, (LAGS, OBS, COLS), (own, near, far, core), smem=1)
    every = lax.all_to_all(spread, TM, 0, 0, tiled=True)
    part = call(
        lag_body,
        (2 * QUAD, OBS * OBS // QUAD // 128, 128),
        (every, shift),
        [
            pltpu.VMEM((LAGS, OBS, 2 * COLS), jnp.bfloat16),
            pltpu.VMEM((LAGS, OBS, 2 * COLS), jnp.bfloat16),
            pltpu.VMEM((2, OBS, OBS), jnp.float32),
        ],
        smem=1,
    )
    part = lax.all_to_all(part, ("xl", "yl", "c"), 0, 0, tiled=True)
    part = call(quad_body, (DEPTH, 1, MINE * OBS), (part,))
    part = lax.all_to_all(part, "z", 0, 0, tiled=True)
    return call(final_body, (MINE, 1, OBS), (part,)).reshape(1, MINE, OBS)


def solution(mesh):
    finer = Mesh(mesh.devices.reshape(2, 2, 2, 16, 2, 2), TM + TILE)
    in_specs = (P(TM, None, TILE, None), P(TILE, None), P(TILE, None), P(TILE, None))
    return jax.shard_map(
        shards, mesh=finer, in_specs=in_specs, out_specs=P(TM, TILE, None), check_vma=False
    )
```

time: 90.7 us -> 88.2 us (0.972)
  waiting for transfers between devices: 7.51 us -> 3.92 us
  local copies, waits for them, and re-layouts: 3.01 us -> 0.97 us
  blocking collectives: 70.8 us -> 72.5 us
  starting transfers between devices: 4.39 us -> 5.51 us
    ppermute x2, waiting for transfers between devices: 7.51 us -> 3.92 us  [the longest x1 3.92 us: shards(): far = lax.ppermute(own, TILE, pairs + [(b, a) for a, b in pairs])]
    unnamed x8 -> x2, local copies, waits for them, and re-layouts: 3.01 us -> 0.97 us
    all_to_all x1, blocking collectives: 29 us -> 30.8 us  [shards(): part = lax.all_to_all(part, 'z', 0, 0, tiled=True)]
    ppermute x2, starting transfers between devices: 4.39 us -> 5.51 us  [the longest x1 3.04 us: shards(): near = lax.ppermute(own, 'c', [(0, 1), (1, 0)])]
    pallas_call x4 -> x5, Pallas kernels: 4.4 us -> 4.3 us  [call(): pl.pallas_call(body, out_shape=jax.ShapeDtypeStruct(shape, jnp.float32),...]
  transfers between devices with their start and end apart: 2 -> 2, of which waited for: 2 -> 1; matrix products, arithmetic and copies ran while one was open for 0% -> 0% of each run, Pallas kernels for 0% -> 0%
where the time goes in v2:
time: 88.2 us; the launch traced here: 87.9 us
  blocking collectives  72.5 us (82%)
  starting transfers between devices  5.51 us (6%)
  Pallas kernels  4.3 us (5%)
  waiting for transfers between devices  3.92 us (4%)
  local copies, waits for them, and re-layouts  0.97 us (1%)
    all_to_all x1, blocking collectives, shards(): part = lax.all_to_all(part, 'z', 0, 0, tiled=True)  30.8 us
    all_to_all x1, blocking collectives, shards(): every = lax.all_to_all(spread, TM, 0, 0, tiled=True)  26 us
    all_to_all x1, blocking collectives, shards(): part = lax.all_to_all(part, ('xl', 'yl', 'c'), 0, 0, tiled=True)  15.7 us
    pallas_call x5, Pallas kernels, call(): pl.pallas_call(body, out_shape=jax.ShapeDtypeStruct(shape, jnp.float32),...  4.3 us
    ppermute x1, waiting for transfers between devices, shards(): far = lax.ppermute(own, TILE, pairs + [(b, a) for a, b in pairs])  3.92 us
    ppermute x1, starting transfers between devices, shards(): near = lax.ppermute(own, 'c', [(0, 1), (1, 0)])  3.04 us
    ppermute x1, starting transfers between devices, shards(): far = lax.ppermute(own, TILE, pairs + [(b, a) for a, b in pairs])  2.47 us
  transfers between devices with their start and end apart: 2, of which 1 were waited for; matrix products, arithmetic and copies ran while one was open for 0% of the time, Pallas kernels for 0%

profile of v2, /device:TPU:32, one launch (start us, length us, event | category | flops | bytes accessed | tf_op | source)
XLA Modules:
  0.0 87.9 jit_solution(3119406114774230273)
XLA Ops:
  0.0 0.7 pad_add_fusion.fields_ref
  0.7 0.0 copy-start
  0.7 1.0 %copy-done = f32[1,320,2,128]{3,2,1,0:T(2,128)S(1)} copy-done((f32[1,320,2,128]{3,2,1,0:T(2,128)S(1)}, f32[1,320,2,128]{3,2,1,0:T(2,128)}, u32[]{:S(2)}) %copy-start) | copy-done | bytes 327704
  1.7 2.5 %collective-permute-start.1 = (f32[648,128]{1,0:T(8,128)S(1)}, f32[648,128]{1,0:T(8,128)S(1)}, u32[]{:S(2)}, u32[]{:S(2)}) collective-permute-start(f32[648,128]{1,0:T(8,128)S(1)} %shard_map.46.own_ref), channel_id=1, source_target_pairs={{1,2},{3,4},{5,6},{7,8},{9,10},{11,12},{13,14},{15,16},{17,18},{19... | collective-permute-start | bytes 995336 | tf_op jit(solution)/shard_map/ppermute | solution.py:162
  4.2 3.0 %collective-permute-start = (f32[648,128]{1,0:T(8,128)S(1)}, f32[648,128]{1,0:T(8,128)S(1)}, u32[]{:S(2)}, u32[]{:S(2)}) collective-permute-start(f32[648,128]{1,0:T(8,128)S(1)} %shard_map.46.own_ref), channel_id=1, source_target_pairs={{0,1},{1,0},{2,3},{3,2},{4,5},{5,4},{6,7},{7,6},{8,9},{9,8},{10,11... | collective-permute-start | bytes 995336 | tf_op jit(solution)/shard_map/ppermute | solution.py:163
  7.2 3.9 %collective-permute-done.1.far_ref = f32[648,128]{1,0:T(8,128)S(1)} collective-permute-done((f32[648,128]{1,0:T(8,128)S(1)}, f32[648,128]{1,0:T(8,128)S(1)}, u32[]{:S(2)}, u32[]{:S(2)}) %collective-permute-start.1) | collective-permute-done | bytes 331808 | tf_op jit(solution)/shard_map/ppermute | solution.py:162
  11.2 0.0 collective-permute-done.near_ref
  11.2 1.0 %shard_map.47 = f32[8,320,128]{2,1,0:T(8,128)S(1)} custom-call(f32[648,128]{1,0:T(8,128)S(1)} %shard_map.46.own_ref, f32[648,128]{1,0:T(8,128)S(1)} %collective-permute-done.near_ref, f32[648,128]{1,0:T(8,128)S(1)} %collective-permute-done.1.far_ref, s32[1]{0:T(128)} %bitcast.2.core_ref), custom_call_target="tpu_custom_call" | custom-call | tf_op jit(solution)/shard_map/pallas_call | solution.py:21
  12.2 26.0 %all_to_all.15.all_ref = f32[8,320,128]{2,1,0:T(8,128)S(1)} all-to-all(f32[8,320,128]{2,1,0:T(8,128)S(1)} %shard_map.47), channel_id=1, replica_groups=mesh['xh'=2,'xl'=2,'yh'=2,'z'=16,'yl'=2,'c'=2] {'xh','xl','yh'}, dimensions={0} | all-to-all | bytes 2621440 | tf_op jit(solution)/shard_map/all_to_all | solution.py:165
  38.1 2.4 %shard_map.48 = f32[8,200,128]{2,1,0:T(8,128)S(1)} custom-call(f32[8,320,128]{2,1,0:T(8,128)S(1)} %all_to_all.15.all_ref, s32[1]{0:T(128)} %bitcast.1.shift_ref), custom_call_target="tpu_custom_call" | custom-call | tf_op jit(solution)/shard_map/pallas_call | solution.py:21
  40.6 15.7 %all_to_all.16.in_ref = f32[8,200,128]{2,1,0:T(8,128)S(1)} all-to-all(f32[8,200,128]{2,1,0:T(8,128)S(1)} %shard_map.48), channel_id=1, replica_groups=mesh['xh'=2,'xl'=2,'yh'=2,'z'=16,'yl'=2,'c'=2] {'xl','yl','c'}, dimensions={0} | all-to-all | bytes 1638400 | tf_op jit(solution)/shard_map/all_to_all | solution.py:177
  56.2 0.2 shard_map.49
  56.4 30.8 %all_to_all.17.in_ref = f32[16,1,1600]{2,1,0:T(1,128)S(1)} all-to-all(f32[16,1,1600]{2,1,0:T(1,128)S(1)} %shard_map.49), channel_id=1, replica_groups=mesh['xh'=2,'xl'=2,'yh'=2,'z'=16,'yl'=2,'c'=2] {'z'}, dimensions={0} | all-to-all | bytes 204800 | tf_op jit(solution)/shard_map/all_to_all | solution.py:179
  87.2 0.7 shard_map.50
  (1 shorter events, 0.0 us)
Async XLA Ops:
  0.7 1.0 %copy-start = (f32[1,320,2,128]{3,2,1,0:T(2,128)S(1)}, f32[1,320,2,128]{3,2,1,0:T(2,128)}, u32[]{:S(2)}) copy-start(f32[1,320,2,128]{3,2,1,0:T(2,128)} %param.4) | copy-start | bytes 983044
  1.7 9.4 %collective-permute-start.1 = (f32[648,128]{1,0:T(8,128)S(1)}, f32[648,128]{1,0:T(8,128)S(1)}, u32[]{:S(2)}, u32[]{:S(2)}) collective-permute-start(f32[648,128]{1,0:T(8,128)S(1)} %shard_map.46.own_ref), channel_id=1, source_target_pairs={{1,2},{3,4},{5,6},{7,8},{9,10},{11,12},{13,14},{15,16},{17,18},{19... | collective-permute-start | bytes 995336 | tf_op jit(solution)/shard_map/ppermute | solution.py:162
  4.2 7.0 %collective-permute-start = (f32[648,128]{1,0:T(8,128)S(1)}, f32[648,128]{1,0:T(8,128)S(1)}, u32[]{:S(2)}, u32[]{:S(2)}) collective-permute-start(f32[648,128]{1,0:T(8,128)S(1)} %shard_map.46.own_ref), channel_id=1, source_target_pairs={{0,1},{1,0},{2,3},{3,2},{4,5},{5,4},{6,7},{7,6},{8,9},{9,8},{10,11... | collective-permute-start | bytes 995336 | tf_op jit(solution)/shard_map/ppermute | solution.py:163

commit v3 on v2

--- a/solution.py
+++ b/solution.py
@@ -1,3 +1,5 @@
+import functools
+
 import jax
 import jax.numpy as jnp
 from jax import lax
@@ -12,6 +14,7 @@
 DEPTH, QUAD = 16, 4
 MINE = OBS // (DEPTH * QUAD)
 PACKED = 648
+HALF = OBS // 2
 
 VM = pl.BlockSpec(memory_space=pltpu.VMEM)
 
@@ -80,7 +83,7 @@
                     out_ref[t, o : o + n, :] = value
 
 
-def lag_body(all_ref, shift_ref, out_ref, hi_ref, lo_ref, acc_ref):
+def split_body(all_ref, shift_ref, core_ref, out_ref, hi_ref, lo_ref):
     for g in range(LAGS):
         full = all_ref[g]
         hi = full.astype(jnp.bfloat16)
@@ -89,35 +92,46 @@
         for ref, value in ((hi_ref, hi), (lo_ref, lo)):
             ref[g, :, 0:COLS] = value
             ref[before, :, COLS : 2 * COLS] = value
-
-    def product(a, b):
-        return lax.dot_general(
-            a, b, (((1,), (1,)), ((), ())), preferred_element_type=jnp.float32
-        )
-
+    lag_rows(1 - core_ref[0], hi_ref, lo_ref, shift_ref, out_ref)
+
+
+def lag_body(hi_ref, lo_ref, shift_ref, core_ref, out_ref):
+    lag_rows(core_ref[0], hi_ref, lo_ref, shift_ref, out_ref)
+
+
+def lag_rows(half, hi_ref, lo_ref, shift_ref, out_ref):
+    rows = pl.ds(pl.multiple_of(half * HALF, HALF), HALF)
     total = None
     for g in range(0, LAGS, 2):
-        hi, lo = hi_ref[g], lo_ref[g]
+        hi, lo = hi_ref[g, rows, :], lo_ref[g, rows, :]
         right = []
         for pick in range(2):
             partner = lax.rem(shift_ref[0] + (2 * pick + g), LAGS)
             hi_p, lo_p = hi_ref[partner], lo_ref[partner]
             right.append(jnp.concatenate([hi_p, lo_p, hi_p], axis=1))
-        term = product(jnp.concatenate([hi, hi, lo], axis=1), jnp.concatenate(right, axis=0))
+        term = lax.dot_general(
+            jnp.concatenate([hi, hi, lo], axis=1),
+            jnp.concatenate(right, axis=0),
+            (((1,), (1,)), ((), ())),
+            preferred_element_type=jnp.float32,
+        )
         total = term if total is None else total + term
-    acc_ref[0] = total[:, 0:OBS]
-    acc_ref[1] = total[:, OBS : 2 * OBS]
-    half = DEPTH // 2 * MINE
+    out_ref[0] = total[:, 0:OBS]
+    out_ref[1] = total[:, OBS : 2 * OBS]
+
+
+def deal_body(mine_ref, other_ref, out_ref, acc_ref):
+    acc_ref[...] = mine_ref[...] + other_ref[...]
+    count = DEPTH // 2 * MINE
     for pick in range(2):
         for q in range(QUAD):
-            to_q = pick * QUAD + q
-            for z in range(DEPTH):
+            for z in range(DEPTH // 2):
                 src = slice((z * QUAD + q) * MINE, (z * QUAD + q + 1) * MINE)
-                to = z * MINE
-                out_ref[to_q, to : to + MINE, :] = acc_ref[pick, src, 0:128]
-                out_ref[to_q, 2 * half + to : 2 * half + to + MINE, :] = acc_ref[pick, src, 128:256]
-                to, side = (to % half) + 4 * half, (to // half) * 64
-                out_ref[to_q, to : to + MINE, side : side + 64] = acc_ref[pick, src, 256:320]
+                chunk, to = pick * QUAD + q, z * MINE
+                out_ref[chunk, to : to + MINE, :] = acc_ref[pick, src, 0:128]
+                out_ref[chunk, count + to : count + to + MINE, :] = acc_ref[pick, src, 128:256]
+                to, side = 2 * count + to % (count // 2), to // (count // 2) * 64
+                out_ref[chunk, to : to + MINE, side : side + 64] = acc_ref[pick, src, 256:320]
 
 
 def summed(parts):
@@ -127,19 +141,18 @@
 
 
 def quad_body(in_ref, out_ref):
-    half = DEPTH // 2 * MINE
-    total = summed([in_ref[i] for i in range(2 * QUAD)])
-    left, mid, last = total[: 2 * half], total[2 * half : 4 * half], total[4 * half :]
-    swapped = pltpu.roll(last, 64, 1)
-    for z in range(DEPTH):
-        to = z * MINE
-        side = last if to < half else swapped
-        for i in range(MINE):
-            row = to + i
+    count = DEPTH // 2 * MINE
+    for c in range(2):
+        total = summed([in_ref[i] for i in range(c, 2 * QUAD, 2)])
+        left, mid, last = total[:count], total[count : 2 * count], total[2 * count :]
+        swapped = pltpu.roll(last, 64, 1)
+        for row in range(count):
+            z, i = c * DEPTH // 2 + row // MINE, row % MINE
+            side = last if row < count // 2 else swapped
+            at = row % (count // 2)
             out_ref[z, :, i * OBS : i * OBS + 128] = left[row : row + 1]
             out_ref[z, :, i * OBS + 128 : i * OBS + 256] = mid[row : row + 1]
-            row = row % half
-            out_ref[z, :, i * OBS + 256 : i * OBS + 320] = side[row : row + 1, 0:64]
+            out_ref[z, :, i * OBS + 256 : i * OBS + 320] = side[at : at + 1, 0:64]
 
 
 def final_body(in_ref, out_ref):
@@ -163,17 +176,20 @@
     near = lax.ppermute(own, "c", [(0, 1), (1, 0)])
     spread = call(smooth_body, (LAGS, OBS, COLS), (own, near, far, core), smem=1)
     every = lax.all_to_all(spread, TM, 0, 0, tiled=True)
-    part = call(
-        lag_body,
-        (2 * QUAD, OBS * OBS // QUAD // 128, 128),
-        (every, shift),
-        [
-            pltpu.VMEM((LAGS, OBS, 2 * COLS), jnp.bfloat16),
-            pltpu.VMEM((LAGS, OBS, 2 * COLS), jnp.bfloat16),
-            pltpu.VMEM((2, OBS, OBS), jnp.float32),
-        ],
-        smem=1,
-    )
+    split = jax.ShapeDtypeStruct((LAGS, OBS, 2 * COLS), jnp.bfloat16)
+    half = jax.ShapeDtypeStruct((2, HALF, OBS), jnp.float32)
+    smem = pl.BlockSpec(memory_space=pltpu.SMEM)
+    other, hi, lo = pl.pallas_call(
+        split_body,
+        out_shape=[half, split, split],
+        in_specs=[VM, smem, smem],
+        out_specs=[VM] * 3,
+        compiler_params=pltpu.CompilerParams(vmem_limit_bytes=16 * 2**20),
+    )(every, shift, core)
+    other = lax.ppermute(other, "c", [(0, 1), (1, 0)])
+    mine = call(lag_body, half.shape, (hi, lo, shift, core), smem=2)
+    chunks = (2 * QUAD, HALF * OBS // QUAD // 128, 128)
+    part = call(deal_body, chunks, (mine, other), [pltpu.VMEM(half.shape, jnp.float32)])
     part = lax.all_to_all(part, ("xl", "yl", "c"), 0, 0, tiled=True)
     part = call(quad_body, (DEPTH, 1, MINE * OBS), (part,))
     part = lax.all_to_all(part, "z", 0, 0, tiled=True)

time: 88.2 us -> 86.9 us (0.985)
  the two profiles are of different devices: /device:TPU:32 before, /device:TPU:2 now
where the time goes in v3:
time: 86.9 us; the launch traced here: 86.6 us
  blocking collectives  66.7 us (77%)
  starting transfers between devices  11.5 us (13%)
  Pallas kernels  5.28 us (6%)
  waiting for transfers between devices  1.31 us (2%)
  local copies, waits for them, and re-layouts  0.97 us (1%)
    all_to_all x1, blocking collectives, shards(): part = lax.all_to_all(part, 'z', 0, 0, tiled=True)  31.8 us
    all_to_all x1, blocking collectives, shards(): every = lax.all_to_all(spread, TM, 0, 0, tiled=True)  22 us
    all_to_all x1, blocking collectives, shards(): part = lax.all_to_all(part, ('xl', 'yl', 'c'), 0, 0, tiled=True)  12.9 us
    ppermute x1, starting transfers between devices, shards(): other = lax.ppermute(other, 'c', [(0, 1), (1, 0)])  6 us
    ppermute x1, starting transfers between devices, shards(): near = lax.ppermute(own, 'c', [(0, 1), (1, 0)])  4.83 us
    pallas_call x6, Pallas kernels, call(): pl.pallas_call(body, out_shape=jax.ShapeDtypeStruct(shape, jnp.float32),...  3.44 us
    pallas_call x1, Pallas kernels, shards(): pl.pallas_call(split_body, out_shape=[half, split, split], in_specs=[VM,...  1.84 us
  transfers between devices with their start and end apart: 3, of which 2 were waited for; matrix products, arithmetic and copies ran while one was open for 0% of the time, Pallas kernels for 2%

profile of v3, /device:TPU:2, one launch (start us, length us, event | category | flops | bytes accessed | tf_op | source)
XLA Modules:
  0.0 86.6 jit_solution(11605065436225902903)
XLA Ops:
  0.0 0.7 pad_add_fusion.fields_ref
  0.7 0.0 copy-start
  0.7 1.0 %copy-done = f32[1,320,2,128]{3,2,1,0:T(2,128)S(1)} copy-done((f32[1,320,2,128]{3,2,1,0:T(2,128)S(1)}, f32[1,320,2,128]{3,2,1,0:T(2,128)}, u32[]{:S(2)}) %copy-start) | copy-done | bytes 327704
  1.7 0.7 collective-permute-start.1
  2.4 4.8 %collective-permute-start = (f32[648,128]{1,0:T(8,128)S(1)}, f32[648,128]{1,0:T(8,128)S(1)}, u32[]{:S(2)}, u32[]{:S(2)}) collective-permute-start(f32[648,128]{1,0:T(8,128)S(1)} %shard_map.46.own_ref), channel_id=1, source_target_pairs={{0,1},{1,0},{2,3},{3,2},{4,5},{5,4},{6,7},{7,6},{8,9},{9,8},{10,11... | collective-permute-start | bytes 995336 | tf_op jit(solution)/shard_map/ppermute | solution.py:176
  7.2 0.0 collective-permute-done.1.far_ref
  7.3 1.2 %collective-permute-done.near_ref = f32[648,128]{1,0:T(8,128)S(1)} collective-permute-done((f32[648,128]{1,0:T(8,128)S(1)}, f32[648,128]{1,0:T(8,128)S(1)}, u32[]{:S(2)}, u32[]{:S(2)}) %collective-permute-start) | collective-permute-done | bytes 331808 | tf_op jit(solution)/shard_map/ppermute | solution.py:176
  8.5 1.0 %shard_map.47 = f32[8,320,128]{2,1,0:T(8,128)S(1)} custom-call(f32[648,128]{1,0:T(8,128)S(1)} %shard_map.46.own_ref, f32[648,128]{1,0:T(8,128)S(1)} %collective-permute-done.near_ref, f32[648,128]{1,0:T(8,128)S(1)} %collective-permute-done.1.far_ref, s32[1]{0:T(128)} %bitcast.2.core_ref), custom_call_target="tpu_custom_call" | custom-call | tf_op jit(solution)/shard_map/pallas_call | solution.py:24
  9.5 22.0 %all_to_all.15.all_ref = f32[8,320,128]{2,1,0:T(8,128)S(1)} all-to-all(f32[8,320,128]{2,1,0:T(8,128)S(1)} %shard_map.47), channel_id=1, replica_groups=mesh['xh'=2,'xl'=2,'yh'=2,'z'=16,'yl'=2,'c'=2] {'xh','xl','yh'}, dimensions={0} | all-to-all | bytes 2621440 | tf_op jit(solution)/shard_map/all_to_all | solution.py:178
  31.5 1.8 %shard_map.48 = (f32[2,160,320]{2,1,0:T(8,128)S(1)}, bf16[8,320,256]{2,1,0:T(8,128)(2,1)S(1)}, bf16[8,320,256]{2,1,0:T(8,128)(2,1)S(1)}) custom-call(f32[8,320,128]{2,1,0:T(8,128)S(1)} %all_to_all.15.all_ref, s32[1]{0:T(128)} %bitcast.1.shift_ref, s32[1]{0:T(128)} %bitcast.2.core_ref), custom_call_target="tpu_custom_call" | custom-call | tf_op jit(solution)/shard_map/pallas_call | solution.py:182
  33.4 6.0 %collective-permute-start.2 = (f32[2,160,320]{2,1,0:T(8,128)S(1)}, f32[2,160,320]{2,1,0:T(8,128)S(1)}, u32[]{:S(2)}, u32[]{:S(2)}) collective-permute-start(f32[2,160,320]{2,1,0:T(8,128)S(1)} %get-tuple-element.16), channel_id=1, source_target_pairs={{0,1},{1,0},{2,3},{3,2},{4,5},{5,4},{6,7},{7,6},{8,9},{9,8},{10,11... | collective-permute-start | bytes 1228808 | tf_op jit(solution)/shard_map/ppermute | solution.py:189
  39.4 1.4 %shard_map.49.mine_ref = f32[2,160,320]{2,1,0:T(8,128)S(1)} custom-call(bf16[8,320,256]{2,1,0:T(8,128)(2,1)S(1)} %get-tuple-element.14.hi_ref, bf16[8,320,256]{2,1,0:T(8,128)(2,1)S(1)} %get-tuple-element.15.lo_ref, s32[1]{0:T(128)} %bitcast.1.shift_ref, s32[1]{0:T(128)} %bitcast.2.core_ref), custom_call_target="tpu_custom_call" | custom-call | tf_op jit(solution)/shard_map/pallas_call | solution.py:24
  40.8 0.1 collective-permute-done.2.other_ref
  40.8 0.2 shard_map.50
  41.0 12.9 %all_to_all.16.in_ref = f32[8,100,128]{2,1,0:T(8,128)S(1)} all-to-all(f32[8,100,128]{2,1,0:T(8,128)S(1)} %shard_map.50), channel_id=1, replica_groups=mesh['xh'=2,'xl'=2,'yh'=2,'z'=16,'yl'=2,'c'=2] {'xl','yl','c'}, dimensions={0} | all-to-all | bytes 819200 | tf_op jit(solution)/shard_map/all_to_all | solution.py:193
  53.9 0.2 shard_map.51
  54.0 31.8 %all_to_all.17.in_ref = f32[16,1,1600]{2,1,0:T(1,128)S(1)} all-to-all(f32[16,1,1600]{2,1,0:T(1,128)S(1)} %shard_map.51), channel_id=1, replica_groups=mesh['xh'=2,'xl'=2,'yh'=2,'z'=16,'yl'=2,'c'=2] {'z'}, dimensions={0} | all-to-all | bytes 204800 | tf_op jit(solution)/shard_map/all_to_all | solution.py:195
  85.9 0.7 shard_map.52
  (1 shorter events, 0.0 us)
Async XLA Ops:
  0.7 1.0 %copy-start = (f32[1,320,2,128]{3,2,1,0:T(2,128)S(1)}, f32[1,320,2,128]{3,2,1,0:T(2,128)}, u32[]{:S(2)}) copy-start(f32[1,320,2,128]{3,2,1,0:T(2,128)} %param.4) | copy-start | bytes 983044
  1.7 5.5 %collective-permute-start.1 = (f32[648,128]{1,0:T(8,128)S(1)}, f32[648,128]{1,0:T(8,128)S(1)}, u32[]{:S(2)}, u32[]{:S(2)}) collective-permute-start(f32[648,128]{1,0:T(8,128)S(1)} %shard_map.46.own_ref), channel_id=1, source_target_pairs={{1,2},{3,4},{5,6},{7,8},{9,10},{11,12},{13,14},{15,16},{17,18},{19... | collective-permute-start | bytes 995336 | tf_op jit(solution)/shard_map/ppermute | solution.py:175
  2.4 6.1 %collective-permute-start = (f32[648,128]{1,0:T(8,128)S(1)}, f32[648,128]{1,0:T(8,128)S(1)}, u32[]{:S(2)}, u32[]{:S(2)}) collective-permute-start(f32[648,128]{1,0:T(8,128)S(1)} %shard_map.46.own_ref), channel_id=1, source_target_pairs={{0,1},{1,0},{2,3},{3,2},{4,5},{5,4},{6,7},{7,6},{8,9},{9,8},{10,11... | collective-permute-start | bytes 995336 | tf_op jit(solution)/shard_map/ppermute | solution.py:176
  33.4 7.5 %collective-permute-start.2 = (f32[2,160,320]{2,1,0:T(8,128)S(1)}, f32[2,160,320]{2,1,0:T(8,128)S(1)}, u32[]{:S(2)}, u32[]{:S(2)}) collective-permute-start(f32[2,160,320]{2,1,0:T(8,128)S(1)} %get-tuple-element.16), channel_id=1, source_target_pairs={{0,1},{1,0},{2,3},{3,2},{4,5},{5,4},{6,7},{7,6},{8,9},{9,8},{10,11... | collective-permute-start | bytes 1228808 | tf_op jit(solution)/shard_map/ppermute | solution.py:189

commit v4 on v3

--- a/solution.py
+++ b/solution.py
@@ -63,7 +63,7 @@
     coef = [row(up_ref, 1), row(own_ref, 0), row(own_ref, 1), row(down_ref, 0)]
     wet = [row(up_ref, 3), row(own_ref, 2), row(own_ref, 3), row(down_ref, 2)]
     late = [row(own_ref, 4), row(own_ref, 5)]
-    n = 32
+    n = 160
     for o in range(0, OBS, n):
         rows = [
             ref[pl.ds(2 * o + r, n, 2), :]
@@ -88,11 +88,8 @@
         full = all_ref[g]
         hi = full.astype(jnp.bfloat16)
         lo = (full - hi.astype(jnp.float32)).astype(jnp.bfloat16)
-        before = (g + LAGS - 1) % LAGS
-        for ref, value in ((hi_ref, hi), (lo_ref, lo)):
-            ref[g, :, 0:COLS] = value
-            ref[before, :, COLS : 2 * COLS] = value
-    lag_rows(1 - core_ref[0], hi_ref, lo_ref, shift_ref, out_ref)
+        hi_ref[g], lo_ref[g] = hi, lo
+    lag_whole(1 - core_ref[0], hi_ref, lo_ref, shift_ref, out_ref)
 
 
 def lag_body(hi_ref, lo_ref, shift_ref, core_ref, out_ref):
@@ -103,11 +100,12 @@
     rows = pl.ds(pl.multiple_of(half * HALF, HALF), HALF)
     total = None
     for g in range(0, LAGS, 2):
-        hi, lo = hi_ref[g, rows, :], lo_ref[g, rows, :]
+        left = [(hi_ref[i, rows, :], lo_ref[i, rows, :]) for i in (g, g + 1)]
+        hi, lo = (jnp.concatenate(pair, axis=1) for pair in zip(*left))
         right = []
         for pick in range(2):
-            partner = lax.rem(shift_ref[0] + (2 * pick + g), LAGS)
-            hi_p, lo_p = hi_ref[partner], lo_ref[partner]
+            at = [lax.rem(shift_ref[0] + (2 * pick + i), LAGS) for i in (g, g + 1)]
+            hi_p, lo_p = (jnp.concatenate([ref[i] for i in at], axis=1) for ref in (hi_ref, lo_ref))
             right.append(jnp.concatenate([hi_p, lo_p, hi_p], axis=1))
         term = lax.dot_general(
             jnp.concatenate([hi, hi, lo], axis=1),
@@ -116,6 +114,24 @@
             preferred_element_type=jnp.float32,
         )
         total = term if total is None else total + term
+    out_ref[0] = total[:, 0:OBS]
+    out_ref[1] = total[:, OBS : 2 * OBS]
+
+
+def lag_whole(half, hi_ref, lo_ref, shift_ref, out_ref):
+    rows = pl.ds(pl.multiple_of(half * HALF, HALF), HALF)
+    hi, lo = (jnp.concatenate([ref[g, rows, :] for g in range(LAGS)], axis=1) for ref in (hi_ref, lo_ref))
+    right = []
+    for pick in range(2):
+        at = [lax.rem(shift_ref[0] + (2 * pick + g), LAGS) for g in range(LAGS)]
+        hi_p, lo_p = (jnp.concatenate([ref[i] for i in at], axis=1) for ref in (hi_ref, lo_ref))
+        right.append(jnp.concatenate([hi_p, lo_p, hi_p], axis=1))
+    total = lax.dot_general(
+        jnp.concatenate([hi, hi, lo], axis=1),
+        jnp.concatenate(right, axis=0),
+        (((1,), (1,)), ((), ())),
+        preferred_element_type=jnp.float32,
+    )
     out_ref[0] = total[:, 0:OBS]
     out_ref[1] = total[:, OBS : 2 * OBS]
 
@@ -176,7 +192,7 @@
     near = lax.ppermute(own, "c", [(0, 1), (1, 0)])
     spread = call(smooth_body, (LAGS, OBS, COLS), (own, near, far, core), smem=1)
     every = lax.all_to_all(spread, TM, 0, 0, tiled=True)
-    split = jax.ShapeDtypeStruct((LAGS, OBS, 2 * COLS), jnp.bfloat16)
+    split = jax.ShapeDtypeStruct((LAGS, OBS, COLS), jnp.bfloat16)
     half = jax.ShapeDtypeStruct((2, HALF, OBS), jnp.float32)
     smem = pl.BlockSpec(memory_space=pltpu.SMEM)
     other, hi, lo = pl.pallas_call(

time: 86.9 us -> 86.1 us (level)
  transfers between devices with their start and end apart: 3 -> 3, of which waited for: 2 -> 1; matrix products, arithmetic and copies ran while one was open for 0% -> 0% of each run, Pallas kernels for 2% -> 2%
where the time goes in v4:
time: 86.1 us; the launch traced here: 85.8 us
  blocking collectives  66.7 us (77%)
  starting transfers between devices  11.5 us (13%)
  Pallas kernels  4.56 us (5%)
  waiting for transfers between devices  1.28 us (1%)
  local copies, waits for them, and re-layouts  0.97 us (1%)
    all_to_all x1, blocking collectives, shards(): part = lax.all_to_all(part, 'z', 0, 0, tiled=True)  31.8 us
    all_to_all x1, blocking collectives, shards(): every = lax.all_to_all(spread, TM, 0, 0, tiled=True)  22 us
    all_to_all x1, blocking collectives, shards(): part = lax.all_to_all(part, ('xl', 'yl', 'c'), 0, 0, tiled=True)  12.9 us
    ppermute x1, starting transfers between devices, shards(): other = lax.ppermute(other, 'c', [(0, 1), (1, 0)])  5.99 us
    ppermute x1, starting transfers between devices, shards(): near = lax.ppermute(own, 'c', [(0, 1), (1, 0)])  4.83 us
    pallas_call x6, Pallas kernels, call(): pl.pallas_call(body, out_shape=jax.ShapeDtypeStruct(shape, jnp.float32),...  3.1 us
  transfers between devices with their start and end apart: 3, of which 1 were waited for; matrix products, arithmetic and copies ran while one was open for 0% of the time, Pallas kernels for 2%

profile of v4, /device:TPU:2, one launch (start us, length us, event | category | flops | bytes accessed | tf_op | source)
XLA Modules:
  0.0 85.8 jit_solution(15597921735072889251)
XLA Ops:
  0.0 0.7 pad_add_fusion.fields_ref
  0.7 0.0 copy-start
  0.7 1.0 %copy-done = f32[1,320,2,128]{3,2,1,0:T(2,128)S(1)} copy-done((f32[1,320,2,128]{3,2,1,0:T(2,128)S(1)}, f32[1,320,2,128]{3,2,1,0:T(2,128)}, u32[]{:S(2)}) %copy-start) | copy-done | bytes 327704
  1.7 0.7 collective-permute-start.1
  2.4 4.8 %collective-permute-start = (f32[648,128]{1,0:T(8,128)S(1)}, f32[648,128]{1,0:T(8,128)S(1)}, u32[]{:S(2)}, u32[]{:S(2)}) collective-permute-start(f32[648,128]{1,0:T(8,128)S(1)} %shard_map.46.own_ref), channel_id=1, source_target_pairs={{0,1},{1,0},{2,3},{3,2},{4,5},{5,4},{6,7},{7,6},{8,9},{9,8},{10,11... | collective-permute-start | bytes 995336 | tf_op jit(solution)/shard_map/ppermute | solution.py:192
  7.2 0.0 collective-permute-done.1.far_ref
  7.3 1.2 %collective-permute-done.near_ref = f32[648,128]{1,0:T(8,128)S(1)} collective-permute-done((f32[648,128]{1,0:T(8,128)S(1)}, f32[648,128]{1,0:T(8,128)S(1)}, u32[]{:S(2)}, u32[]{:S(2)}) %collective-permute-start) | collective-permute-done | bytes 331808 | tf_op jit(solution)/shard_map/ppermute | solution.py:192
  8.5 0.6 shard_map.47
  9.1 22.0 %all_to_all.15.all_ref = f32[8,320,128]{2,1,0:T(8,128)S(1)} all-to-all(f32[8,320,128]{2,1,0:T(8,128)S(1)} %shard_map.47), channel_id=1, replica_groups=mesh['xh'=2,'xl'=2,'yh'=2,'z'=16,'yl'=2,'c'=2] {'xh','xl','yh'}, dimensions={0} | all-to-all | bytes 2621440 | tf_op jit(solution)/shard_map/all_to_all | solution.py:194
  31.1 1.5 %shard_map.48 = (f32[2,160,320]{2,1,0:T(8,128)S(1)}, bf16[8,320,128]{2,1,0:T(8,128)(2,1)S(1)}, bf16[8,320,128]{2,1,0:T(8,128)(2,1)S(1)}) custom-call(f32[8,320,128]{2,1,0:T(8,128)S(1)} %all_to_all.15.all_ref, s32[1]{0:T(128)} %bitcast.1.shift_ref, s32[1]{0:T(128)} %bitcast.2.core_ref), custom_call_target="tpu_custom_call" | custom-call | tf_op jit(solution)/shard_map/pallas_call | solution.py:198
  32.6 6.0 %collective-permute-start.2 = (f32[2,160,320]{2,1,0:T(8,128)S(1)}, f32[2,160,320]{2,1,0:T(8,128)S(1)}, u32[]{:S(2)}, u32[]{:S(2)}) collective-permute-start(f32[2,160,320]{2,1,0:T(8,128)S(1)} %get-tuple-element.16), channel_id=1, source_target_pairs={{0,1},{1,0},{2,3},{3,2},{4,5},{5,4},{6,7},{7,6},{8,9},{9,8},{10,11... | collective-permute-start | bytes 1228808 | tf_op jit(solution)/shard_map/ppermute | solution.py:205
  38.6 1.4 %shard_map.49.mine_ref = f32[2,160,320]{2,1,0:T(8,128)S(1)} custom-call(bf16[8,320,128]{2,1,0:T(8,128)(2,1)S(1)} %get-tuple-element.14.hi_ref, bf16[8,320,128]{2,1,0:T(8,128)(2,1)S(1)} %get-tuple-element.15.lo_ref, s32[1]{0:T(128)} %bitcast.1.shift_ref, s32[1]{0:T(128)} %bitcast.2.core_ref), custom_call_target="tpu_custom_call" | custom-call | tf_op jit(solution)/shard_map/pallas_call | solution.py:24
  40.0 0.0 collective-permute-done.2.other_ref
  40.1 0.2 shard_map.50
  40.2 12.9 %all_to_all.16.in_ref = f32[8,100,128]{2,1,0:T(8,128)S(1)} all-to-all(f32[8,100,128]{2,1,0:T(8,128)S(1)} %shard_map.50), channel_id=1, replica_groups=mesh['xh'=2,'xl'=2,'yh'=2,'z'=16,'yl'=2,'c'=2] {'xl','yl','c'}, dimensions={0} | all-to-all | bytes 819200 | tf_op jit(solution)/shard_map/all_to_all | solution.py:209
  53.1 0.2 shard_map.51
  53.3 31.8 %all_to_all.17.in_ref = f32[16,1,1600]{2,1,0:T(1,128)S(1)} all-to-all(f32[16,1,1600]{2,1,0:T(1,128)S(1)} %shard_map.51), channel_id=1, replica_groups=mesh['xh'=2,'xl'=2,'yh'=2,'z'=16,'yl'=2,'c'=2] {'z'}, dimensions={0} | all-to-all | bytes 204800 | tf_op jit(solution)/shard_map/all_to_all | solution.py:211
  85.1 0.7 shard_map.52
  (1 shorter events, 0.0 us)
Async XLA Ops:
  0.7 1.0 %copy-start = (f32[1,320,2,128]{3,2,1,0:T(2,128)S(1)}, f32[1,320,2,128]{3,2,1,0:T(2,128)}, u32[]{:S(2)}) copy-start(f32[1,320,2,128]{3,2,1,0:T(2,128)} %param.4) | copy-start | bytes 983044
  1.7 5.5 %collective-permute-start.1 = (f32[648,128]{1,0:T(8,128)S(1)}, f32[648,128]{1,0:T(8,128)S(1)}, u32[]{:S(2)}, u32[]{:S(2)}) collective-permute-start(f32[648,128]{1,0:T(8,128)S(1)} %shard_map.46.own_ref), channel_id=1, source_target_pairs={{1,2},{3,4},{5,6},{7,8},{9,10},{11,12},{13,14},{15,16},{17,18},{19... | collective-permute-start | bytes 995336 | tf_op jit(solution)/shard_map/ppermute | solution.py:191
  2.4 6.1 %collective-permute-start = (f32[648,128]{1,0:T(8,128)S(1)}, f32[648,128]{1,0:T(8,128)S(1)}, u32[]{:S(2)}, u32[]{:S(2)}) collective-permute-start(f32[648,128]{1,0:T(8,128)S(1)} %shard_map.46.own_ref), channel_id=1, source_target_pairs={{0,1},{1,0},{2,3},{3,2},{4,5},{5,4},{6,7},{7,6},{8,9},{9,8},{10,11... | collective-permute-start | bytes 995336 | tf_op jit(solution)/shard_map/ppermute | solution.py:192
  32.6 7.5 %collective-permute-start.2 = (f32[2,160,320]{2,1,0:T(8,128)S(1)}, f32[2,160,320]{2,1,0:T(8,128)S(1)}, u32[]{:S(2)}, u32[]{:S(2)}) collective-permute-start(f32[2,160,320]{2,1,0:T(8,128)S(1)} %get-tuple-element.16), channel_id=1, source_target_pairs={{0,1},{1,0},{2,3},{3,2},{4,5},{5,4},{6,7},{7,6},{8,9},{9,8},{10,11... | collective-permute-start | bytes 1228808 | tf_op jit(solution)/shard_map/ppermute | solution.py:205

commit v5 on v4

--- a/solution.py
+++ b/solution.py
@@ -31,14 +31,6 @@
     )(*args)
 
 
-def pack_body(block_ref, fields_ref, out_ref):
-    wet = fields_ref[2:4, :]
-    both = jnp.concatenate([wet] * 4, axis=0)
-    for i in range(0, 2 * OBS, 8):
-        out_ref[i : i + 8, :] = block_ref[i : i + 8, :] * both
-    out_ref[2 * OBS :, :] = fields_ref[...]
-
-
 def smooth_body(own_ref, near_ref, far_ref, core_ref, out_ref):
     @pl.when(core_ref[0] == 0)
     def _():
@@ -61,20 +53,20 @@
         return ref[2 * OBS + i : 2 * OBS + i + 1, :]
 
     coef = [row(up_ref, 1), row(own_ref, 0), row(own_ref, 1), row(down_ref, 0)]
-    wet = [row(up_ref, 3), row(own_ref, 2), row(own_ref, 3), row(down_ref, 2)]
+    wet = [row(ref, 2 + r) for ref in (up_ref, own_ref, down_ref) for r in (0, 1)]
     late = [row(own_ref, 4), row(own_ref, 5)]
     n = 160
     for o in range(0, OBS, n):
         rows = [
-            ref[pl.ds(2 * o + r, n, 2), :]
-            for ref in (up_ref, own_ref, down_ref)
+            ref[pl.ds(2 * o + r, n, 2), :] * wet[2 * i + r]
+            for i, ref in enumerate((up_ref, own_ref, down_ref))
             for r in (0, 1)
         ]
         first = []
         for i in range(4):
             mid = rows[i + 1]
             total = coef[i] * mid + 0.2 * (rows[i] + rows[i + 2]) + lateral(mid)
-            first.append(total * wet[i])
+            first.append(total * wet[i + 1])
         for r in range(2):
             mid = first[r + 1]
             value = late[r] * mid + 0.2 * (first[r] + first[r + 2]) + lateral(mid)
@@ -178,11 +170,11 @@
 
 
 def shards(blocks, coef_first, coef_second, wet):
-    fields = (coef_first, wet, coef_second)
-    fields = sum(
-        jnp.pad(f, ((2 * i, 6 - 2 * i), (0, 0))).astype(jnp.float32) for i, f in enumerate(fields)
-    )
-    own = call(pack_body, (PACKED, COLS), (blocks.reshape(2 * OBS, COLS), fields), limit=4)
+    own = jnp.pad(blocks[0], ((0, (PACKED - 2 * OBS) // 2), (0, 0), (0, 0)))
+    for i, field in enumerate((coef_first, wet, coef_second)):
+        room = ((OBS + i, 3 - i), (0, 0), (0, 0))
+        own = own + jnp.pad(field[None], room).astype(jnp.float32)
+    own = own.reshape(PACKED, COLS)
     shift = 4 * lax.axis_index("xh") + lax.axis_index("yh")
     shift = shift.astype(jnp.int32).reshape(1)
     core = lax.axis_index("c").astype(jnp.int32).reshape(1)

time: 86.1 us -> 85.4 us (level)
  the two profiles are of different devices: /device:TPU:2 before, /device:TPU:32 now
where the time goes in v5:
time: 85.4 us; the launch traced here: 85 us
  blocking collectives  66.4 us (78%)
  starting transfers between devices  9.08 us (11%)
  Pallas kernels  4.51 us (5%)
  waiting for transfers between devices  3.97 us (5%)
  other arithmetic  1.04 us (1%)
    all_to_all x1, blocking collectives, shards(): part = lax.all_to_all(part, 'z', 0, 0, tiled=True)  29.7 us
    all_to_all x1, blocking collectives, shards(): every = lax.all_to_all(spread, TM, 0, 0, tiled=True)  26 us
    all_to_all x1, blocking collectives, shards(): part = lax.all_to_all(part, ('xl', 'yl', 'c'), 0, 0, tiled=True)  10.7 us
    ppermute x1, waiting for transfers between devices, shards(): far = lax.ppermute(own, TILE, pairs + [(b, a) for a, b in pairs])  3.92 us
    ppermute x1, starting transfers between devices, shards(): other = lax.ppermute(other, 'c', [(0, 1), (1, 0)])  3.57 us
    pallas_call x5, Pallas kernels, call(): pl.pallas_call(body, out_shape=jax.ShapeDtypeStruct(shape, jnp.float32),...  3.05 us
    ppermute x1, starting transfers between devices, shards(): near = lax.ppermute(own, 'c', [(0, 1), (1, 0)])  3.04 us
    ppermute x1, starting transfers between devices, shards(): far = lax.ppermute(own, TILE, pairs + [(b, a) for a, b in pairs])  2.47 us
  transfers between devices with their start and end apart: 3, of which 1 were waited for; matrix products, arithmetic and copies ran while one was open for 0% of the time, Pallas kernels for 2%

profile of v5, /device:TPU:32, one launch (start us, length us, event | category | flops | bytes accessed | tf_op | source)
XLA Modules:
  0.0 85.0 jit_solution(382165807949381444)
XLA Ops:
  0.0 1.0 %pad_add_fusion = f32[324,2,128]{2,1,0:T(2,128)S(1)} fusion(f32[1,2,128]{2,1,0:T(2,128)} %bitcast.12, s32[1,2,128]{2,1,0:T(2,128)} %bitcast.13, f32[1,2,128]{2,1,0:T(2,128)} %bitcast.14, f32[320,2,128]{2,1,0:T(2,128)} %bitcast.11), kind=kLoop, calls=%fused_computation | loop fusion | flops 331776 | bytes 662528 | tf_op jit(solution)/shard_map/add | solution.py:176
  1.0 2.5 %collective-permute-start.1 = (f32[648,128]{1,0:T(8,128)S(1)}, f32[648,128]{1,0:T(8,128)S(1)}, u32[]{:S(2)}, u32[]{:S(2)}) collective-permute-start(f32[648,128]{1,0:T(8,128)S(1)} %bitcast.8), channel_id=1, source_target_pairs={{1,2},{3,4},{5,6},{7,8},{9,10},{11,12},{13,14},{15,16},{17,18},{19... | collective-permute-start | bytes 995336 | tf_op jit(solution)/shard_map/ppermute | solution.py:183
  3.5 3.0 %collective-permute-start = (f32[648,128]{1,0:T(8,128)S(1)}, f32[648,128]{1,0:T(8,128)S(1)}, u32[]{:S(2)}, u32[]{:S(2)}) collective-permute-start(f32[648,128]{1,0:T(8,128)S(1)} %bitcast.9), channel_id=1, source_target_pairs={{0,1},{1,0},{2,3},{3,2},{4,5},{5,4},{6,7},{7,6},{8,9},{9,8},{10,11... | collective-permute-start | bytes 995336 | tf_op jit(solution)/shard_map/ppermute | solution.py:184
  6.6 3.9 %collective-permute-done.1.far_ref = f32[648,128]{1,0:T(8,128)S(1)} collective-permute-done((f32[648,128]{1,0:T(8,128)S(1)}, f32[648,128]{1,0:T(8,128)S(1)}, u32[]{:S(2)}, u32[]{:S(2)}) %collective-permute-start.1) | collective-permute-done | bytes 331808 | tf_op jit(solution)/shard_map/ppermute | solution.py:183
  10.5 0.0 collective-permute-done.near_ref
  10.5 0.6 shard_map.46
  11.1 26.0 %all_to_all.15.all_ref = f32[8,320,128]{2,1,0:T(8,128)S(1)} all-to-all(f32[8,320,128]{2,1,0:T(8,128)S(1)} %shard_map.46), channel_id=1, replica_groups=mesh['xh'=2,'xl'=2,'yh'=2,'z'=16,'yl'=2,'c'=2] {'xh','xl','yh'}, dimensions={0} | all-to-all | bytes 2621440 | tf_op jit(solution)/shard_map/all_to_all | solution.py:186
  37.1 1.5 %shard_map.47 = (f32[2,160,320]{2,1,0:T(8,128)S(1)}, bf16[8,320,128]{2,1,0:T(8,128)(2,1)S(1)}, bf16[8,320,128]{2,1,0:T(8,128)(2,1)S(1)}) custom-call(f32[8,320,128]{2,1,0:T(8,128)S(1)} %all_to_all.15.all_ref, s32[1]{0:T(128)} %bitcast.5.shift_ref, s32[1]{0:T(128)} %bitcast.6.core_ref), custom_call_target="tpu_custom_call" | custom-call | tf_op jit(solution)/shard_map/pallas_call | solution.py:190
  38.6 3.6 %collective-permute-start.2 = (f32[2,160,320]{2,1,0:T(8,128)S(1)}, f32[2,160,320]{2,1,0:T(8,128)S(1)}, u32[]{:S(2)}, u32[]{:S(2)}) collective-permute-start(f32[2,160,320]{2,1,0:T(8,128)S(1)} %get-tuple-element.16), channel_id=1, source_target_pairs={{0,1},{1,0},{2,3},{3,2},{4,5},{5,4},{6,7},{7,6},{8,9},{9,8},{10,11... | collective-permute-start | bytes 1228808 | tf_op jit(solution)/shard_map/ppermute | solution.py:197
  42.1 1.4 %shard_map.48.mine_ref = f32[2,160,320]{2,1,0:T(8,128)S(1)} custom-call(bf16[8,320,128]{2,1,0:T(8,128)(2,1)S(1)} %get-tuple-element.14.hi_ref, bf16[8,320,128]{2,1,0:T(8,128)(2,1)S(1)} %get-tuple-element.15.lo_ref, s32[1]{0:T(128)} %bitcast.5.shift_ref, s32[1]{0:T(128)} %bitcast.6.core_ref), custom_call_target="tpu_custom_call" | custom-call | tf_op jit(solution)/shard_map/pallas_call | solution.py:24
  43.5 0.0 collective-permute-done.2.other_ref
  43.6 0.2 shard_map.49
  43.8 10.7 %all_to_all.16.in_ref = f32[8,100,128]{2,1,0:T(8,128)S(1)} all-to-all(f32[8,100,128]{2,1,0:T(8,128)S(1)} %shard_map.49), channel_id=1, replica_groups=mesh['xh'=2,'xl'=2,'yh'=2,'z'=16,'yl'=2,'c'=2] {'xl','yl','c'}, dimensions={0} | all-to-all | bytes 819200 | tf_op jit(solution)/shard_map/all_to_all | solution.py:201
  54.5 0.2 shard_map.50
  54.6 29.7 %all_to_all.17.in_ref = f32[16,1,1600]{2,1,0:T(1,128)S(1)} all-to-all(f32[16,1,1600]{2,1,0:T(1,128)S(1)} %shard_map.50), channel_id=1, replica_groups=mesh['xh'=2,'xl'=2,'yh'=2,'z'=16,'yl'=2,'c'=2] {'z'}, dimensions={0} | all-to-all | bytes 204800 | tf_op jit(solution)/shard_map/all_to_all | solution.py:203
  84.4 0.7 shard_map.51
Async XLA Ops:
  1.0 9.4 %collective-permute-start.1 = (f32[648,128]{1,0:T(8,128)S(1)}, f32[648,128]{1,0:T(8,128)S(1)}, u32[]{:S(2)}, u32[]{:S(2)}) collective-permute-start(f32[648,128]{1,0:T(8,128)S(1)} %bitcast.8), channel_id=1, source_target_pairs={{1,2},{3,4},{5,6},{7,8},{9,10},{11,12},{13,14},{15,16},{17,18},{19... | collective-permute-start | bytes 995336 | tf_op jit(solution)/shard_map/ppermute | solution.py:183
  3.5 7.0 %collective-permute-start = (f32[648,128]{1,0:T(8,128)S(1)}, f32[648,128]{1,0:T(8,128)S(1)}, u32[]{:S(2)}, u32[]{:S(2)}) collective-permute-start(f32[648,128]{1,0:T(8,128)S(1)} %bitcast.9), channel_id=1, source_target_pairs={{0,1},{1,0},{2,3},{3,2},{4,5},{5,4},{6,7},{7,6},{8,9},{9,8},{10,11... | collective-permute-start | bytes 995336 | tf_op jit(solution)/shard_map/ppermute | solution.py:184
  38.6 5.0 %collective-permute-start.2 = (f32[2,160,320]{2,1,0:T(8,128)S(1)}, f32[2,160,320]{2,1,0:T(8,128)S(1)}, u32[]{:S(2)}, u32[]{:S(2)}) collective-permute-start(f32[2,160,320]{2,1,0:T(8,128)S(1)} %get-tuple-element.16), channel_id=1, source_target_pairs={{0,1},{1,0},{2,3},{3,2},{4,5},{5,4},{6,7},{7,6},{8,9},{9,8},{10,11... | collective-permute-start | bytes 1228808 | tf_op jit(solution)/shard_map/ppermute | solution.py:197
